TPU v7x, 32 devices: a whole 2x2x4 slice. The times are simulated.
32 devices in a mesh: wide: 4 (over y, core), narrow: 8 (over z, x).
Axes of the slice: x: 2, y: 2, z: 4, core: 2. Of those that a mesh axis runs over, the one named last changes fastest.
Arguments:
- tokens: bfloat16 [16384, 1280], P(('wide', 'narrow')), may hold values from -6 to 6
- lengths: int32 [8, 4], P('wide'), may hold values from 1 to 1280, 1920 in all within a row
- qkv_weight: bfloat16 [3, 1280, 1280], P(None, 'wide', 'narrow'), may hold values from -0.15625 to 0.15625
- out_weight: bfloat16 [1280, 1280], P('narrow', 'wide'), may hold values from -0.625 to 0.625
- up_weight: bfloat16 [1280, 1280], P('wide', 'narrow'), may hold values from -0.15625 to 0.15625
- up_bias: bfloat16 [1280], P('narrow'), may hold values from -3 to 3
- down_weight: bfloat16 [1280, 1280], P('narrow', 'wide'), may hold values from -0.15625 to 0.15625
- down_bias: bfloat16 [1280], replicated, may hold values from -3 to 3
- attn_gain: float32 [1280], replicated, may hold values from 0.5 to 1.5
- mlp_gain: float32 [1280], replicated, may hold values from 0.5 to 1.5
- query_scale: float32 [80], replicated, may hold values from 0 to 1.5
- cotangent: bfloat16 [16384, 1280], P(('wide', 'narrow')), may hold values from -6 to 6
Outputs:
- result: bfloat16 [16384, 1280], P(('wide', 'narrow'))
- tokens_grad: float32 [16384, 1280], P(('wide', 'narrow'))
- qkv_grad: float32 [3, 1280, 1280], P(None, 'wide', 'narrow')
- out_grad: float32 [1280, 1280], P('narrow', 'wide')
- up_grad: float32 [1280, 1280], P('wide', 'narrow')
- up_bias_grad: float32 [1280], P('narrow')
- down_grad: float32 [1280, 1280], P('narrow', 'wide')
- down_bias_grad: float32 [1280], replicated
- attn_gain_grad: float32 [1280], replicated
- mlp_gain_grad: float32 [1280], replicated
- query_scale_grad: float32 [80], replicated
Inputs may be any that keep to these rules, and one draw needn't show every extreme that they name: Each row holds 4 document lengths that sum to 1920; the longest is exactly 1280; the last 128 tokens of every sequence are padding.
All inputs are finite; a program needn't handle non-finite values.
Results may differ from a plain program's by a relative error of at most 0.012.
The roundings to bfloat16 on the way count: a program that leaves them out, or rounds other values in their place, can miss the bound.
Values may be sent and summed in bfloat16 or wider, within the bound.
A program may use at most 320 MiB of HBM per device.

v0:
```python
import math

import jax
import jax.numpy as jnp
from jax import lax
from jax.sharding import PartitionSpec as P

HEAD_DIM = 80
LEN = 2048
WINDOW = 1024
BLOCK = 512
NDOC = 4


LOG_TWO_E = 1.4426950408889634
EPSILON = 1e-06
NEG_FILL = -1e30


def group_rows(values):
    return lax.all_gather(values, "narrow", axis=0, tiled=True)


def group_parts(values):
    return lax.psum_scatter(values, "narrow", scatter_dimension=0, tiled=True)


def contract_last(left, right):
    return lax.dot_general(
        left, right, (((1,), (1,)), ((), ())), preferred_element_type=jnp.float32
    )


def contract_first(left, right):
    return lax.dot_general(
        left, right, (((0,), (0,)), ((), ())), preferred_element_type=jnp.float32
    )


def norm_share(inputs, norm_gain):
    inverse = lax.rsqrt(jnp.mean(inputs * inputs, axis=1) + EPSILON)
    normed = inputs * inverse[:, None]
    return (inverse, normed, (normed * norm_gain).astype(jnp.bfloat16))


def norm_back(grad_normal, norm_gain, inverse, normed):
    scaled = grad_normal * norm_gain
    inner_dots = jnp.mean(scaled * normed, axis=1)
    grad_inputs = inverse[:, None] * (scaled - normed * inner_dots[:, None])
    return (grad_inputs, jnp.sum(grad_normal * normed, axis=0))


def segment_ids(lengths_row):
    positions = jnp.arange(LEN, dtype=jnp.int32)
    ends = jnp.cumsum(lengths_row)
    return jnp.sum((positions[:, None] >= ends[None, :]).astype(jnp.int32), axis=1)


def block_mask(segments, padded_seg, offset):
    query_pos = offset + jnp.arange(BLOCK, dtype=jnp.int32)
    key_pos = offset - WINDOW + jnp.arange(WINDOW + BLOCK, dtype=jnp.int32)
    query_seg = segments[offset : offset + BLOCK]
    key_seg = padded_seg[offset : offset + WINDOW + BLOCK]
    spacing = query_pos[:, None] - key_pos[None, :]
    same_doc = query_seg[:, None] == key_seg[None, :]
    inside = (spacing >= 0) & (spacing < WINDOW)
    real_doc = (query_seg[:, None] < NDOC) | (spacing == 0)
    return same_doc & inside & real_doc


def padded_inputs(keys_in, values_in, segments):
    pad_rows = jnp.zeros((WINDOW,) + keys_in.shape[1:], keys_in.dtype)
    keys_pad = jnp.concatenate([pad_rows, keys_in], axis=0)
    values_pad = jnp.concatenate([pad_rows, values_in], axis=0)
    padded_seg = jnp.concatenate([jnp.full((WINDOW,), -2, jnp.int32), segments])
    return (keys_pad, values_pad, padded_seg)


def attend_forward(queries, keys_in, values_in, segments):
    keys_pad, values_pad, padded_seg = padded_inputs(keys_in, values_in, segments)
    outputs = []
    logsums = []
    for block_index in range(LEN // BLOCK):
        offset = block_index * BLOCK
        query_block = queries[offset : offset + BLOCK]
        key_block = keys_pad[offset : offset + WINDOW + BLOCK]
        value_block = values_pad[offset : offset + WINDOW + BLOCK]
        allowed = block_mask(segments, padded_seg, offset)
        scores = jnp.einsum(
            "ihd,jhd->hij", query_block, key_block, preferred_element_type=jnp.float32
        )
        masked = jnp.where(allowed[None], scores, NEG_FILL)
        maxima = jnp.max(masked, axis=2)
        exponent = jnp.exp(masked - maxima[:, :, None])
        totals = jnp.sum(exponent, axis=2)
        probs_low = (exponent / totals[:, :, None]).astype(jnp.bfloat16)
        block_out = jnp.einsum(
            "hij,jhd->ihd", probs_low, value_block, preferred_element_type=jnp.float32
        )
        outputs.append(block_out.astype(jnp.bfloat16))
        logsums.append(maxima + jnp.log(totals))
    return (jnp.concatenate(outputs, axis=0), jnp.concatenate(logsums, axis=1))


def attend_backward(queries, keys_in, values_in, segments, logsum, grad_out):
    keys_pad, values_pad, padded_seg = padded_inputs(keys_in, values_in, segments)
    grad_keys = jnp.zeros(keys_pad.shape, jnp.float32)
    grad_values = jnp.zeros(values_pad.shape, jnp.float32)
    grad_queries = []
    for block_index in range(LEN // BLOCK):
        offset = block_index * BLOCK
        query_block = queries[offset : offset + BLOCK]
        key_block = keys_pad[offset : offset + WINDOW + BLOCK]
        value_block = values_pad[offset : offset + WINDOW + BLOCK]
        grad_block = grad_out[offset : offset + BLOCK]
        allowed = block_mask(segments, padded_seg, offset)
        scores = jnp.einsum(
            "ihd,jhd->hij", query_block, key_block, preferred_element_type=jnp.float32
        )
        masked = jnp.where(allowed[None], scores, NEG_FILL)
        soft_probs = jnp.exp(masked - logsum[:, offset : offset + BLOCK, None])
        probs_low = soft_probs.astype(jnp.bfloat16)
        grad_probs = jnp.einsum(
            "ihd,jhd->hij", grad_block, value_block, preferred_element_type=jnp.float32
        )
        inner_sums = jnp.sum(soft_probs * grad_probs, axis=2)
        grad_scores = (soft_probs * (grad_probs - inner_sums[:, :, None])).astype(jnp.bfloat16)
        grad_queries.append(
            jnp.einsum("hij,jhd->ihd", grad_scores, key_block, preferred_element_type=jnp.float32)
        )
        key_terms = jnp.einsum(
            "hij,ihd->jhd", grad_scores, query_block, preferred_element_type=jnp.float32
        )
        value_terms = jnp.einsum(
            "hij,ihd->jhd", probs_low, grad_block, preferred_element_type=jnp.float32
        )
        grad_keys = grad_keys.at[offset : offset + WINDOW + BLOCK].add(key_terms)
        grad_values = grad_values.at[offset : offset + WINDOW + BLOCK].add(value_terms)
    return (jnp.concatenate(grad_queries, axis=0), grad_keys[WINDOW:], grad_values[WINDOW:])


def silu_slope(hidden_pre):
    sigmoid_pre = jax.nn.sigmoid(hidden_pre)
    return sigmoid_pre * (1.0 + hidden_pre * (1.0 - sigmoid_pre))


def per_device(
    tokens,
    lengths,
    qkv_weight,
    out_weight,
    up_weight,
    up_bias,
    down_weight,
    down_bias,
    attn_gain,
    mlp_gain,
    query_scale,
    cotangent,
):
    head_count = qkv_weight.shape[2] // HEAD_DIM
    seq_count = lengths.shape[0]
    row_count = seq_count * LEN

    def by_sequence(values):
        return values.reshape((seq_count, LEN) + values.shape[1:])

    qkv_full, out_full, up_full, down_full = (
        lax.all_gather(qkv_weight, "wide", axis=1, tiled=True),
        lax.all_gather(out_weight, "wide", axis=1, tiled=True),
        lax.all_gather(up_weight, "wide", axis=0, tiled=True),
        lax.all_gather(down_weight, "wide", axis=1, tiled=True),
    )
    segments = jax.vmap(segment_ids)(lengths)
    inputs = tokens.astype(jnp.float32)
    inverse_one, normed_one, normal_one = norm_share(inputs, attn_gain)
    rows_one = group_rows(normal_one)
    projected = jnp.einsum("td,cdn->ctn", rows_one, qkv_full, preferred_element_type=jnp.float32)
    scale_dim = LOG_TWO_E / math.sqrt(HEAD_DIM) * jax.nn.softplus(query_scale)
    query_heads = projected[0].reshape(row_count, head_count, HEAD_DIM)
    query_low = (query_heads * scale_dim).astype(jnp.bfloat16)
    key_low = projected[1].astype(jnp.bfloat16).reshape(row_count, head_count, HEAD_DIM)
    value_low = projected[2].astype(jnp.bfloat16).reshape(row_count, head_count, HEAD_DIM)
    attended, logsum = jax.vmap(attend_forward)(
        by_sequence(query_low), by_sequence(key_low), by_sequence(value_low), segments
    )
    attended_rows = attended.reshape(row_count, head_count * HEAD_DIM)
    middle = inputs + group_parts(
        jnp.dot(attended_rows, out_full, preferred_element_type=jnp.float32)
    )
    inverse_two, normed_two, normal_two = norm_share(middle, mlp_gain)
    grad_down_bias = jnp.sum(cotangent.astype(jnp.float32), axis=0)
    rows_two = group_rows(normal_two)
    hidden_pre = jnp.dot(rows_two, up_full, preferred_element_type=jnp.float32) + up_bias
    hidden_low = jax.nn.silu(hidden_pre).astype(jnp.bfloat16)
    branch_two = (
        group_parts(jnp.dot(hidden_low, down_full, preferred_element_type=jnp.float32)) + down_bias
    )
    result = middle + branch_two
    grad_rows = group_rows(cotangent)
    grad_hidden = contract_last(grad_rows, down_full)
    grad_pre = (grad_hidden * silu_slope(hidden_pre)).astype(jnp.bfloat16)
    grad_up = contract_first(rows_two, grad_pre)
    grad_down = contract_first(hidden_low, grad_rows)
    grad_up_bias = jnp.sum(grad_pre.astype(jnp.float32), axis=0)
    grad_normal_two = group_parts(contract_last(grad_pre, up_full))
    grad_middle_norm, grad_mlp_gain = norm_back(grad_normal_two, mlp_gain, inverse_two, normed_two)
    grad_middle = cotangent.astype(jnp.float32) + grad_middle_norm
    grad_branch = group_rows(grad_middle.astype(jnp.bfloat16))
    grad_attended = contract_last(grad_branch, out_full).astype(jnp.bfloat16)
    grad_out = contract_first(attended_rows, grad_branch)
    grad_scaled, grad_key, grad_value = jax.vmap(attend_backward)(
        by_sequence(query_low),
        by_sequence(key_low),
        by_sequence(value_low),
        segments,
        logsum,
        by_sequence(grad_attended.reshape(row_count, head_count, HEAD_DIM)),
    )
    grad_scaled = grad_scaled.reshape(row_count, head_count, HEAD_DIM)
    grad_scale_part = (
        jnp.sum(grad_scaled * query_heads, axis=(0, 1))
        * (LOG_TWO_E / math.sqrt(HEAD_DIM))
        * jax.nn.sigmoid(query_scale)
    )
    grad_projected = jnp.stack(
        [
            (grad_scaled * scale_dim).reshape(row_count, head_count * HEAD_DIM),
            grad_key.reshape(row_count, head_count * HEAD_DIM),
            grad_value.reshape(row_count, head_count * HEAD_DIM),
        ]
    ).astype(jnp.bfloat16)
    grad_qkv = jnp.einsum(
        "td,ctn->cdn", rows_one, grad_projected, preferred_element_type=jnp.float32
    )
    grad_normal_one = group_parts(
        jnp.einsum("ctn,cdn->td", grad_projected, qkv_full, preferred_element_type=jnp.float32)
    )
    grad_input_norm, grad_attn_gain = norm_back(grad_normal_one, attn_gain, inverse_one, normed_one)
    grad_tokens = grad_middle + grad_input_norm
    grad_qkv, grad_out, grad_up, grad_down = (
        lax.psum_scatter(grad_qkv, "wide", scatter_dimension=1, tiled=True),
        lax.psum_scatter(grad_out, "wide", scatter_dimension=1, tiled=True),
        lax.psum_scatter(grad_up, "wide", scatter_dimension=0, tiled=True),
        lax.psum_scatter(grad_down, "wide", scatter_dimension=1, tiled=True),
    )
    grad_attn_gain, grad_mlp_gain, grad_down_bias, grad_scale = lax.psum(
        (grad_attn_gain, grad_mlp_gain, grad_down_bias, grad_scale_part), ("wide", "narrow")
    )
    grad_up_bias = lax.psum(grad_up_bias, "wide")
    return (
        result.astype(jnp.bfloat16),
        grad_tokens,
        grad_qkv,
        grad_out,
        grad_up,
        grad_up_bias,
        grad_down,
        grad_down_bias,
        grad_attn_gain,
        grad_mlp_gain,
        grad_scale,
    )


def solution(mesh):
    return jax.shard_map(
        per_device,
        mesh=mesh,
        in_specs=(
            P(("wide", "narrow"), None),
            P("wide", None),
            P(None, "wide", "narrow"),
            P("narrow", "wide"),
            P("wide", "narrow"),
            P("narrow"),
            P("narrow", "wide"),
            P(),
            P(),
            P(),
            P(),
            P(("wide", "narrow"), None),
        ),
        out_specs=(
            P(("wide", "narrow"), None),
            P(("wide", "narrow"), None),
            P(None, "wide", "narrow"),
            P("narrow", "wide"),
            P("wide", "narrow"),
            P("narrow"),
            P("narrow", "wide"),
            P(),
            P(),
            P(),
            P(),
        ),
        check_vma=False,
    )
```

profile of v0, /device:TPU:11, one launch (start us, length us, event | category | flops | bytes accessed | tf_op | source)
XLA Modules:
  0.0 2440.2 jit_solution(1154442507606865514)
XLA Ops:
  41.6 145.9 %all-gather.9.cloned.1.call-done = bf16[4096,1280]{1,0:T(8,128)(2,1)} async-done(((bf16[512,1280]{1,0:T(8,128)(2,1)}), bf16[4096,1280]{1,0:T(8,128)(2,1)}) %all-gather.9.cloned.1.call-update) | async-done | bytes 10485776 | tf_op jit(solution)/shard_map/all_gather | solution.py:21
  273.1 8.6 fusion.161
  281.8 343.2 %reduce-scatter.17.cloned.1.call-done = f32[512,1280]{1,0:T(8,128)} async-done(((f32[4096,1280]{1,0:T(8,128)}), f32[512,1280]{1,0:T(8,128)}) %reduce-scatter.17.cloned.1.call-update) | async-done | bytes 2621456 | tf_op jit(solution)/shard_map/reduce_scatter | solution.py:25
  649.5 129.6 %all-gather.13.cloned.1.call-done = bf16[4096,1280]{1,0:T(8,128)(2,1)} async-done(((bf16[512,1280]{1,0:T(8,128)(2,1)}), bf16[4096,1280]{1,0:T(8,128)(2,1)}) %all-gather.13.cloned.1.call-update) | async-done | bytes 10485776 | tf_op jit(solution)/shard_map/all_gather | solution.py:21
  779.1 9.0 convolution_add_fusion
  788.1 142.1 %all-gather.15.cloned.1.call-done = bf16[4096,1280]{1,0:T(8,128)(2,1)} async-done(((bf16[512,1280]{1,0:T(8,128)(2,1)}), bf16[4096,1280]{1,0:T(8,128)(2,1)}) %all-gather.15.cloned.1.call-update) | async-done | bytes 10485776 | tf_op jit(solution)/shard_map/all_gather | solution.py:21
  930.2 9.2 convert_reduce_fusion.1
  940.4 8.6 fusion.162
  949.1 343.2 %reduce-scatter.21.cloned.1.call-done = f32[512,1280]{1,0:T(8,128)} async-done(((f32[4096,1280]{1,0:T(8,128)}), f32[512,1280]{1,0:T(8,128)}) %reduce-scatter.21.cloned.1.call-update) | async-done | bytes 2621456 | tf_op jit(solution)/shard_map/reduce_scatter | solution.py:25
  1300.7 10.1 convolution_bitcast_fusion.5
  1312.2 9.6 fusion.163
  1321.9 126.4 %all-gather.17.cloned.1.call-done = bf16[4096,1280]{1,0:T(8,128)(2,1)} async-done(((bf16[512,1280]{1,0:T(8,128)(2,1)}), bf16[4096,1280]{1,0:T(8,128)(2,1)}) %all-gather.17.cloned.1.call-update) | async-done | bytes 10485776 | tf_op jit(solution)/shard_map/all_gather | solution.py:21
  1448.3 8.6 convolution_convert_fusion
  1472.3 10.2 multiply_reduce_fusion.3
  1511.7 10.5 multiply_reduce_fusion.1
  1553.1 10.5 multiply_convert_fusion
  1568.3 10.1 multiply_convert_fusion.1
  1618.8 9.8 convolution_bitcast_fusion.6
  1632.1 9.2 fusion.39
  1654.2 12.0 convolution_bitcast_fusion
  1668.2 8.8 fusion.156
  1699.6 340.7 %reduce-scatter.23.cloned.1.call-done = f32[512,1280]{1,0:T(8,128)} async-done(((f32[4096,1280]{1,0:T(8,128)}), f32[512,1280]{1,0:T(8,128)}) %reduce-scatter.23.cloned.1.call-update) | async-done | bytes 2621456 | tf_op jit(solution)/shard_map/reduce_scatter | solution.py:25
  2043.1 343.1 %reduce-scatter.19.cloned.1.call-done = f32[512,1280]{1,0:T(8,128)} async-done(((f32[4096,1280]{1,0:T(8,128)}), f32[512,1280]{1,0:T(8,128)}) %reduce-scatter.19.cloned.1.call-update) | async-done | bytes 2621456 | tf_op jit(solution)/shard_map/reduce_scatter | solution.py:25
  2392.4 40.9 %all-reduce.5 = (f32[1280]{0:T(1024)}, f32[1280]{0:T(1024)}, f32[1280]{0:T(1024)}, f32[80]{0:T(128)}) all-reduce(f32[1280]{0:T(1024)S(1)} %get-tuple-element.123, f32[1280]{0:T(1024)S(1)} %get-tuple-element.109, f32[1280]{0:T(1024)S(1)} %copy-done.61, ...), channel_id=1, replica_groups=mesh['wide'=4,'narrow'=8] {'wide','narrow'}, use_global_device_ids=true, to_apply=%region_29.30 | all-reduce | flops 3920 | bytes 31360 | tf_op jit(solution)/shard_map/psum | solution.py:247
  (350 shorter events, 325.0 us)
Async XLA Ops:
  7.2 30.5 %all-gather.11.cloned.1.call-start = ((), (), s32[]{:S(2)}) async-start(), calls=%async_computation.9 | async-start | bytes 3276800 | tf_op jit(solution)/shard_map/all_gather | solution.py:169
  9.5 178.0 %all-gather.9.cloned.1.call-start = ((), (), s32[]{:S(2)}) async-start(), calls=%async_computation.8 | async-start | bytes 11796480 | tf_op jit(solution)/shard_map/all_gather | solution.py:21
  13.3 611.7 %reduce-scatter.17.cloned.1.call-start = ((), (), s32[]{:S(2)}) async-start(), calls=%async_computation.10 | async-start | bytes 23592960 | tf_op jit(solution)/shard_map/reduce_scatter | solution.py:25
  21.6 250.5 %copy-start.37 = (bf16[1280,160]{0,1:T(8,128)(2,1)}, bf16[1280,160]{0,1:T(8,128)(2,1)S(1)}, u32[]{:S(2)}) copy-start(bf16[1280,160]{0,1:T(8,128)(2,1)S(1)} %reshape.650) | copy-start | bytes 1228804
  32.4 199.3 %copy-start.7 = (pred[2,512,1536]{2,1,0:T(8,128)(4,1)}, pred[2,512,1536]{2,1,0:T(8,128)(4,1)S(1)}, u32[]{:S(2)}) copy-start(pred[2,512,1536]{2,1,0:T(8,128)(4,1)S(1)} %get-tuple-element.168) | copy-start | bytes 4718596
  281.8 347.2 %copy-start.50 = (f32[1280]{0:T(1024)S(1)}, f32[1280]{0:T(1024)}, u32[]{:S(2)}) copy-start(f32[1280]{0:T(1024)} %param.37) | copy-start | bytes 15364
  281.8 497.3 %all-gather.13.cloned.1.call-start = ((), (), s32[]{:S(2)}) async-start(), calls=%async_computation.11 | async-start | bytes 11796480 | tf_op jit(solution)/shard_map/all_gather | solution.py:21
  627.5 668.8 %copy-start.58 = (f32[512]{0:T(512)}, f32[512]{0:T(512)S(1)}, u32[]{:S(2)}) copy-start(f32[512]{0:T(512)S(1)} %add_rsqrt_fusion) | copy-start | bytes 6148
  630.4 299.8 %all-gather.15.cloned.1.call-start = ((), (), s32[]{:S(2)}) async-start(), calls=%async_computation.13 | async-start | bytes 11796480 | tf_op jit(solution)/shard_map/all_gather | solution.py:21
  631.0 661.4 %reduce-scatter.21.cloned.1.call-start = ((), (), s32[]{:S(2)}) async-start(), calls=%async_computation.14 | async-start | bytes 23592960 | tf_op jit(solution)/shard_map/reduce_scatter | solution.py:25
  949.1 499.2 %all-gather.17.cloned.1.call-start = ((), (), s32[]{:S(2)}) async-start(), calls=%async_computation.15 | async-start | bytes 11796480 | tf_op jit(solution)/shard_map/all_gather | solution.py:21
  1299.6 385.6 %reduce-scatter.31.cloned.1.call-start = ((), (), s32[]{:S(2)}) async-start(), calls=%async_computation.20 | async-start | bytes 1638400
  1310.9 376.1 %reduce-scatter.29.cloned.1.call-start = ((), (), s32[]{:S(2)}) async-start(), calls=%async_computation.19 | async-start | bytes 1638400
  1321.9 367.1 %reduce-scatter.27.cloned.1.call-start = ((), (), s32[]{:S(2)}) async-start(), calls=%async_computation.18 | async-start | bytes 1638400
  1628.6 65.9 %reduce-scatter.25.cloned.1.call-start = ((), (), s32[]{:S(2)}) async-start(), calls=%async_computation.17 | async-start | bytes 3276800
  1652.5 387.8 %reduce-scatter.23.cloned.1.call-start = ((), (), s32[]{:S(2)}) async-start(), calls=%async_computation.16 | async-start | bytes 23592960 | tf_op jit(solution)/shard_map/reduce_scatter | solution.py:25
  1666.2 720.0 %reduce-scatter.19.cloned.1.call-start = ((), (), s32[]{:S(2)}) async-start(), calls=%async_computation.12 | async-start | bytes 23592960 | tf_op jit(solution)/shard_map/reduce_scatter | solution.py:25
  1686.9 353.3 %copy-start.56 = (f32[1280]{0:T(1024)S(1)}, f32[1280]{0:T(1024)}, u32[]{:S(2)}) copy-start(f32[1280]{0:T(1024)} %param.36) | copy-start | bytes 15364
  1686.9 353.3 %copy-start.69 = (f32[512]{0:T(512)S(1)}, f32[512]{0:T(512)}, u32[]{:S(2)}) copy-start(f32[512]{0:T(512)} %copy-done.68) | copy-start | bytes 6148
  1697.2 689.0 %copy-start.6 = (f32[512,1280]{1,0:T(8,128)S(1)}, f32[512,1280]{1,0:T(8,128)}, u32[]{:S(2)}) copy-start(f32[512,1280]{1,0:T(8,128)} %copy-done.4) | copy-start | bytes 7864324
  1697.2 689.0 %copy-start.51 = (f32[1280]{0:T(1024)S(1)}, f32[1280]{0:T(1024)}, u32[]{:S(2)}) copy-start(f32[1280]{0:T(1024)} %param.37) | copy-start | bytes 15364
  1697.2 689.0 %copy-start.59 = (f32[512]{0:T(512)S(1)}, f32[512]{0:T(512)}, u32[]{:S(2)}) copy-start(f32[512]{0:T(512)} %copy-done.58) | copy-start | bytes 6148
  1697.2 689.0 %copy-start.71 = (f32[512]{0:T(512)S(1)}, f32[512]{0:T(512)}, u32[]{:S(2)}) copy-start(f32[512]{0:T(512)} %copy-done.70) | copy-start | bytes 6148
  2043.1 349.3 %copy-start.61 = (f32[1280]{0:T(1024)S(1)}, f32[1280]{0:T(1024)}, u32[]{:S(2)}) copy-start(f32[1280]{0:T(1024)} %get-tuple-element.107) | copy-start | bytes 15364
  (88 other events, 1298.8 us)
Sparse Core Ops, SparseCore 0:
  10.2 27.0 all-gather.10
  40.1 147.3 all-gather.8
  281.9 343.0 reduce-scatter.16
  630.5 148.5 all-gather.12
  781.1 149.0 all-gather.14
  949.2 343.1 reduce-scatter.20
  1299.7 148.5 all-gather.16
  1450.8 27.7 reduce-scatter.30
  1481.4 26.5 reduce-scatter.28
  1628.7 28.1 reduce-scatter.26
  1659.6 34.8 reduce-scatter.24
  1698.2 341.9 reduce-scatter.22
  2044.1 342.0 reduce-scatter.18
where the time goes:
time: 2450 us; the launch traced here: 2440 us
  waiting for transfers between devices  1920 us (78%)
  matrix products  228 us (9%)
  local copies, waits for them, and re-layouts  109 us (4%)
  other arithmetic  97.3 us (4%)
  blocking collectives  71 us (3%)
    reduce_scatter x4, waiting for transfers between devices, group_parts(): return lax.psum_scatter(values, 'narrow', scatter_dimension=0, tiled=True)  1370 us
    all_gather x4, waiting for transfers between devices, group_rows(): return lax.all_gather(values, 'narrow', axis=0, tiled=True)  544 us
    unnamed x210, local copies, waits for them, and re-layouts  50.7 us
  transfers between devices with their start and end apart: 13, of which 9 were waited for; matrix products, arithmetic and copies ran while one was open for 12% of the time, Pallas kernels for 0%

commit v1 on v0

--- a/solution.py
+++ b/solution.py
@@ -1,8 +1,11 @@
+import functools
 import math
 
 import jax
 import jax.numpy as jnp
 from jax import lax
+from jax.experimental import pallas as pl
+from jax.experimental.pallas import tpu as pltpu
 from jax.sharding import PartitionSpec as P
 
 HEAD_DIM = 80
@@ -10,11 +13,16 @@
 WINDOW = 1024
 BLOCK = 512
 NDOC = 4
-
+TILE = 256
 
 LOG_TWO_E = 1.4426950408889634
 EPSILON = 1e-06
 NEG_FILL = -1e30
+
+F32 = jnp.float32
+LOW = jnp.bfloat16
+MESH = pl.DeviceIdType.MESH
+VMEM_LIMIT = 62 * 2**20
 
 
 def group_rows(values):
@@ -144,7 +152,7 @@
     return sigmoid_pre * (1.0 + hidden_pre * (1.0 - sigmoid_pre))
 
 
-def per_device(
+def general_device(
     tokens,
     lengths,
     qkv_weight,
@@ -263,7 +271,1107 @@
     )
 
 
+def product(left, right, left_dim=1, right_dim=0):
+    return lax.dot_general(
+        left, right, (((left_dim,), (right_dim,)), ((), ())), preferred_element_type=F32
+    )
+
+
+def flip(value, mask):
+    bit = 1
+    while bit <= mask:
+        if mask & bit:
+            value = value + bit * (1 - 2 * lax.rem(lax.div(value, bit), 2))
+        bit *= 2
+    return value
+
+
+def part(start, size):
+    return pl.ds(pl.multiple_of(start * size, size), size)
+
+
+def chunks(total, size, body):
+    def step(index, carry):
+        body(part(index, size))
+        return carry
+
+    lax.fori_loop(0, total // size, step, 0)
+
+
+def add_rows(target, source, size):
+    def body(span):
+        target[span, :] = (target[span, :].astype(F32) + source[span, :].astype(F32)).astype(LOW)
+
+    chunks(source.shape[0], size, body)
+
+
+class Place:
+    def __init__(self, group):
+        self.wide = lax.axis_index("wide")
+        self.narrow = lax.axis_index("narrow")
+        self.core = lax.rem(self.wide, 2)
+        self.y = lax.div(self.wide, 2)
+        self.quarter = lax.rem(self.narrow, group)
+        self.half = lax.div(self.narrow, group)
+
+    def along_wide(self, mask):
+        return (flip(self.wide, mask), self.narrow)
+
+    def along_narrow(self, mask):
+        return (self.wide, flip(self.narrow, mask))
+
+
+def greet(place, narrow_masks, wide_masks):
+    barrier = pltpu.get_barrier_semaphore()
+    peers = [place.along_narrow(m) for m in narrow_masks]
+    peers += [place.along_wide(m) for m in wide_masks]
+    for peer in peers:
+        pl.semaphore_signal(barrier, inc=1, device_id=peer, device_id_type=MESH)
+    pl.semaphore_wait(barrier, len(peers))
+
+
+def document_ends(lengths, row):
+    ends, total = [], 0
+    for index in range(NDOC):
+        total = total + lengths[row, index]
+        ends.append(total)
+    return ends
+
+
+def first_key(ends, offset):
+    position = offset + lax.broadcasted_iota(jnp.int32, (1, TILE), 1)
+    start = jnp.zeros_like(position)
+    for end in ends:
+        start = jnp.where(position >= end, end, start)
+    start = jnp.maximum(start, position - (WINDOW - 1))
+    return jnp.where(position >= ends[-1], position, start), position
+
+
+def allowed_scores(scores, key_start, offset, first, position):
+    key = key_start + lax.broadcasted_iota(jnp.int32, scores.shape, 0)
+    allowed = key >= first
+    if key_start + scores.shape[0] > offset:
+        allowed = allowed & (key <= position)
+    return jnp.where(allowed, scores, NEG_FILL)
+
+
+def tile_keys(tile):
+    offset = tile * TILE
+    return offset, range(max(0, offset - WINDOW), offset + TILE, TILE)
+
+
+def pipelined(count, first_half, second_half):
+    waiting = None
+    for tile in range(count):
+        current = (tile, first_half(tile))
+        if waiting is not None:
+            second_half(*waiting)
+        waiting = current
+    second_half(*waiting)
+
+
+def attend_head(head, ends, queries, keys, values_t, attended, logsum):
+    def first_half(tile):
+        offset, starts = tile_keys(tile)
+        first, position = first_key(ends, offset)
+        query = queries[head, :, offset : offset + TILE]
+        blocks, maxima = [], None
+        for start in starts:
+            scores = product(keys[head, start : start + TILE, :], query)
+            scores = allowed_scores(scores, start, offset, first, position)
+            top = jnp.max(scores, axis=0, keepdims=True)
+            maxima = top if maxima is None else jnp.maximum(maxima, top)
+            blocks.append(scores)
+        return blocks, maxima
+
+    def second_half(tile, held):
+        blocks, maxima = held
+        offset, starts = tile_keys(tile)
+        total, output = None, None
+        for scores, start in zip(blocks, starts):
+            exponent = jnp.exp(scores - maxima)
+            share = jnp.sum(exponent, axis=0, keepdims=True)
+            term = product(values_t[head, :, start : start + TILE], exponent.astype(LOW))
+            total, output = (
+                (share, term) if total is None else (total + share, output + term)
+            )
+        attended[head, :, offset : offset + TILE] = (output * (1.0 / total)).astype(LOW)
+        logsum[head, :, offset : offset + TILE] = maxima + jnp.log(total)
+
+    pipelined(LEN // TILE, first_half, second_half)
+
+
+def norm_rows(inputs):
+    return lax.rsqrt(jnp.mean(inputs * inputs, axis=1, keepdims=True) + EPSILON)
+
+
+def forward_kernel(
+    group,
+    lengths,
+    tokens,
+    shards,
+    gain,
+    scale,
+    bias,
+    x_out,
+    qf_out,
+    q_out,
+    kt_out,
+    kn_out,
+    vn_out,
+    wq_out,
+    lse_out,
+    att_out,
+    wm_out,
+    bias_out,
+    x_all,
+    w_qkv,
+    w_mlp,
+    w_pair,
+    w_half,
+    bias_all,
+    query_full,
+    query_t,
+    key_t,
+    value_t,
+    key_n,
+    value_n,
+    logsum,
+    attended,
+    att_all,
+    send_sem,
+    recv_sem,
+    local_sem,
+):
+    place = Place(group)
+    core, y, quarter, half, narrow = (
+        place.core,
+        place.y,
+        place.quarter,
+        place.half,
+        place.narrow,
+    )
+    rows = tokens.shape[0]
+    mid = rows // 2
+    slab = shards.shape[1] // 2
+    pair_cols = 2 * shards.shape[2]
+    cols_y = part(y, pair_cols)
+    cols_other = part(1 - y, pair_cols)
+    x_dev, z_dev, far_dev = (
+        place.along_narrow(1),
+        place.along_narrow(2),
+        place.along_narrow(group),
+    )
+    core_dev, y_dev = place.along_wide(1), place.along_wide(2)
+    ids = iter(range(send_sem.shape[0]))
+    sent = []
+
+    def copy(source, target, device, index=None):
+        index = next(ids) if index is None else index
+        return pltpu.make_async_remote_copy(
+            src_ref=source,
+            dst_ref=target,
+            send_sem=send_sem.at[index],
+            recv_sem=recv_sem.at[index],
+            device_id=device,
+            device_id_type=MESH,
+        )
+
+    def exchange(source, target, incoming, device):
+        index = next(ids)
+        out = copy(source, target, device, index)
+        out.start()
+        sent.append(out)
+        return copy(incoming, incoming, device, index)
+
+    greet(place, range(1, 2 * group), (1, 2))
+
+    halves = (slice(0, mid), slice(mid, rows))
+
+    def x_part(mask, which):
+        return x_all.at[flip(quarter, mask), halves[which]]
+
+    w_arrived = exchange(shards.at[:, part(1 - core, slab), :], w_half, w_half, core_dev)
+    x_from = {}
+    for key, device, mask, which in (
+        ("x0", x_dev, 1, 0),
+        ("z1", z_dev, 2, 1),
+        ("x1", x_dev, 1, 1),
+        ("z0", z_dev, 2, 0),
+    ):
+        x_from[key] = exchange(
+            tokens.at[halves[which]], x_part(0, which), x_part(mask, which), device
+        )
+    bias_from = [
+        exchange(bias, bias_all.at[narrow], bias_all.at[flip(narrow, mask)], place.along_narrow(mask))
+        for mask in range(1, 2 * group)
+    ]
+    bias_all[narrow] = bias[...]
+    x_all[quarter] = tokens[...]
+
+    w_arrived.wait_recv()
+    own = shards[:, part(core, slab), :]
+    other = w_half[...]
+    w_pair[:, :, : pair_cols // 2] = jnp.where(core == 0, own, other)
+    w_pair[:, :, pair_cols // 2 :] = jnp.where(core == 0, other, own)
+    for m in range(3):
+        w_qkv[m, core, half, :, cols_y] = w_pair[m]
+        w_mlp[m, core, part(narrow, slab), cols_y] = w_pair[3 + m]
+
+    def q_block(which, columns):
+        return w_qkv.at[:, core, which, :, columns]
+
+    def m_block(m, mask):
+        return w_mlp.at[m, core, part(flip(narrow, mask), slab), cols_y]
+
+    q_far = exchange(q_block(half, cols_y), q_block(half, cols_y), q_block(1 - half, cols_y), far_dev)
+    m_far = [
+        exchange(m_block(m, 0), m_block(m, 0), m_block(m, group), far_dev) for m in range(3)
+    ]
+    q_far.wait_recv()
+    q_y = exchange(
+        w_qkv.at[:, core, :, :, cols_y],
+        w_qkv.at[:, core, :, :, cols_y],
+        w_qkv.at[:, core, :, :, cols_other],
+        y_dev,
+    )
+
+    def z_step(m):
+        m_far[m].wait_recv()
+        return [
+            exchange(m_block(m, o), m_block(m, o), m_block(m, o ^ 2), z_dev) for o in (0, group)
+        ]
+
+    def x_step(m, arrived):
+        for one in arrived:
+            one.wait_recv()
+        return [
+            exchange(m_block(m, o), m_block(m, o), m_block(m, o ^ 1), x_dev)
+            for o in (0, 2, group, group + 2)
+        ]
+
+    m_z = [z_step(0)]
+    x_from["x0"].wait_recv()
+    x_from["d0"] = exchange(x_part(1, 0), x_part(1, 0), x_part(3, 0), z_dev)
+    x_from["z1"].wait_recv()
+    x_from["d1"] = exchange(x_part(2, 1), x_part(2, 1), x_part(3, 1), x_dev)
+    q_y.wait_recv()
+    q_core = exchange(w_qkv.at[:, core], w_qkv.at[:, core], w_qkv.at[:, 1 - core], core_dev)
+    m_z += [z_step(1), z_step(2)]
+    m_x = [x_step(0, m_z[0])]
+    q_core.wait_recv()
+
+    def project(mask):
+        where = flip(quarter, mask)
+        span = part(where, rows)
+        inputs = x_all[where].astype(F32)
+        normal = (inputs * norm_rows(inputs) * gain[...]).astype(LOW)
+        weight = w_qkv[...].reshape(-1, normal.shape[1])
+        result = product(weight, normal, 1, 1)
+        size = result.shape[0] // 3
+        heads = size // HEAD_DIM
+        query_full[:, span] = result[:size]
+        query_t[:, :, span] = (
+            (result[:size] * scale[...]).astype(LOW).reshape(heads, HEAD_DIM, rows)
+        )
+        key = result[size : 2 * size].astype(LOW).reshape(heads, HEAD_DIM, rows)
+        value = result[2 * size :].astype(LOW).reshape(heads, HEAD_DIM, rows)
+        key_t[:, :, span] = key
+        value_t[:, :, span] = value
+        for head in range(heads):
+            key_n[head, span, :] = key[head].T
+            value_n[head, span, :] = value[head].T
+
+    project(0)
+    x_from["x1"].wait_recv()
+    project(1)
+    x_from["z0"].wait_recv()
+    project(2)
+    x_from["d0"].wait_recv()
+    x_from["d1"].wait_recv()
+    project(3)
+    m_x += [x_step(1, m_z[1]), x_step(2, m_z[2])]
+
+    stores = []
+
+    def store(source, target):
+        one = pltpu.make_async_copy(source, target, local_sem.at[len(stores)])
+        one.start()
+        stores.append(one)
+
+    store(x_all, x_out)
+    store(query_full, qf_out)
+    store(query_t, q_out)
+    store(key_t, kt_out)
+    store(key_n, kn_out)
+    store(value_n, vn_out)
+    store(w_qkv, wq_out)
+
+    ends = document_ends(lengths, half)
+    heads = query_t.shape[0]
+    first_id = next(ids)
+    for _ in range(3 * heads - 1):
+        next(ids)
+
+    def att_copy(head, mask, incoming):
+        peer = flip(quarter, mask)
+        index = first_id + 3 * head + mask - 1
+        slot = (lax.div(head, 2), lax.rem(head, 2))
+        if incoming:
+            there = att_all.at[slot[0], slot[1], peer]
+            return copy(there, there, place.along_narrow(mask), index)
+        return copy(
+            attended.at[head, :, part(peer, rows)],
+            att_all.at[slot[0], slot[1], quarter],
+            place.along_narrow(mask),
+            index,
+        )
+
+    def y_step(m):
+        for one in m_x[m]:
+            one.wait_recv()
+        return exchange(
+            w_mlp.at[m, core, :, cols_y],
+            w_mlp.at[m, core, :, cols_y],
+            w_mlp.at[m, core, :, cols_other],
+            y_dev,
+        )
+
+    def core_step(m, arrived):
+        arrived.wait_recv()
+        return exchange(w_mlp.at[m, core], w_mlp.at[m, core], w_mlp.at[m, 1 - core], core_dev)
+
+    m_y = [y_step(0)]
+
+    def one_head(head, carry):
+        attend_head(head, ends, query_t, key_n, value_t, attended, logsum)
+        for mask in (3, 1, 2):
+            att_copy(head, mask, False).start()
+        att_all[lax.div(head, 2), lax.rem(head, 2), quarter] = attended[head, :, part(quarter, rows)]
+        return carry
+
+    lax.fori_loop(0, heads // 2, one_head, 0)
+    m_y.append(y_step(1))
+    lax.fori_loop(heads // 2, heads, one_head, 0)
+    m_y.append(y_step(2))
+    m_core = [core_step(0, m_y[0]), core_step(1, m_y[1])]
+    store(logsum, lse_out)
+
+    def finish_head(head, carry):
+        for mask in (1, 2, 3):
+            att_copy(head, mask, True).wait_recv()
+        return carry
+
+    lax.fori_loop(0, heads, finish_head, 0)
+    store(att_all, att_out)
+    for one in bias_from:
+        one.wait_recv()
+    store(bias_all, bias_out)
+    m_core.append(core_step(2, m_y[2]))
+    for m in range(3):
+        m_core[m].wait_recv()
+        store(w_mlp.at[m], wm_out.at[m])
+
+    def finish_send(head, carry):
+        for mask in (1, 2, 3):
+            att_copy(head, mask, False).wait_send()
+        return carry
+
+    lax.fori_loop(0, heads, finish_send, 0)
+    for one in sent:
+        one.wait_send()
+    for one in stores:
+        one.wait()
+
+
+def mlp_kernel(
+    tokens,
+    attended,
+    weights,
+    up_bias,
+    down_bias,
+    gain,
+    cotangent,
+    result,
+    grad_middle,
+    grad_attended,
+    grads,
+    sums,
+):
+    att = attended[...].reshape(-1, attended.shape[-1])
+    size = att.shape[0]
+    wide_shape = (2, size // 2, weights.shape[-1])
+
+    def weight(m):
+        return weights[m].reshape(size, -1)
+
+    middle = tokens[...].astype(F32) + product(att, weight(0), 0, 0)
+    inverse = norm_rows(middle)
+    normed = middle * inverse
+    normal = (normed * gain[...]).astype(LOW)
+    pre = product(normal, weight(1), 1, 1) + up_bias[...]
+    gate = 1.0 / (1.0 + jnp.exp(-pre))
+    hidden = (pre * gate).astype(LOW)
+    cot = cotangent[...]
+    grad_hidden = product(cot, weight(2), 1, 1)
+    grad_pre = (grad_hidden * (gate * (1.0 + pre * (1.0 - gate)))).astype(LOW)
+    result[...] = (middle + (product(hidden, weight(2)) + down_bias[...])).astype(LOW)
+    grad_normal = product(grad_pre, weight(1))
+    scaled = grad_normal * gain[...]
+    inner = jnp.mean(scaled * normed, axis=1, keepdims=True)
+    cot_full = cot.astype(F32)
+    grad_mid = cot_full + inverse * (scaled - normed * inner)
+    grad_middle[...] = grad_mid
+    branch = grad_mid.astype(LOW)
+    grad_attended[...] = product(weight(0), branch, 1, 1).astype(LOW).reshape(grad_attended.shape)
+    grads[0] = product(att, branch).astype(LOW).reshape(wide_shape)
+    grads[1] = product(grad_pre, normal, 0, 0).astype(LOW).reshape(wide_shape)
+    grads[2] = product(hidden, cot, 0, 0).astype(LOW).reshape(wide_shape)
+    sums[...] = jnp.zeros_like(sums)
+    sums[0:1, :] = jnp.sum(grad_normal * normed, axis=0, keepdims=True)
+    sums[1:2, :] = jnp.sum(cot_full, axis=0, keepdims=True)
+    sums[2:3, :] = jnp.sum(grad_pre.astype(F32), axis=0, keepdims=True)
+
+
+def backward_head(
+    head,
+    ends,
+    queries,
+    query_full,
+    keys,
+    keys_t,
+    values,
+    grad_out,
+    logsum,
+    scale,
+    grads_t,
+    sum_keys,
+    sum_values,
+    sum_scale,
+):
+    sum_keys[...] = jnp.zeros_like(sum_keys)
+    sum_values[...] = jnp.zeros_like(sum_values)
+
+    def first_half(tile):
+        offset, starts = tile_keys(tile)
+        first, position = first_key(ends, offset)
+        span = slice(offset, offset + TILE)
+        query, grad, log_row = queries[head, :, span], grad_out[head, :, span], logsum[head, :, span]
+        blocks, inner = [], None
+        for start in starts:
+            scores = product(keys[head, start : start + TILE, :], query)
+            scores = allowed_scores(scores, start, offset, first, position)
+            probs = jnp.exp(scores - log_row)
+            grad_probs = product(values[head, start : start + TILE, :], grad)
+            share = jnp.sum(probs * grad_probs, axis=0, keepdims=True)
+            inner = share if inner is None else inner + share
+            blocks.append((probs, grad_probs))
+        return blocks, inner, query, grad
+
+    def second_half(tile, held):
+        blocks, inner, query, grad = held
+        offset, starts = tile_keys(tile)
+        span = slice(offset, offset + TILE)
+        grad_scaled = None
+        for (probs, grad_probs), start in zip(blocks, starts):
+            there = slice(start, start + TILE)
+            grad_scores = (probs * (grad_probs - inner)).astype(LOW)
+            term = product(keys_t[head, :, there], grad_scores)
+            grad_scaled = term if grad_scaled is None else grad_scaled + term
+            sum_keys[:, there] += product(query, grad_scores, 1, 1)
+            sum_values[:, there] += product(grad, probs.astype(LOW), 1, 1)
+        grads_t[0, head, :, span] = (grad_scaled * scale[...]).astype(LOW)
+        terms = grad_scaled * query_full[part(head, HEAD_DIM), span]
+        sum_scale[...] += terms[:, : TILE // 2] + terms[:, TILE // 2 :]
+
+    pipelined(LEN // TILE, first_half, second_half)
+    grads_t[1, head] = sum_keys[...].astype(LOW)
+    grads_t[2, head] = sum_values[...].astype(LOW)
+
+
+def backward_kernel(
+    group,
+    lengths,
+    tokens,
+    gain,
+    scale,
+    sums,
+    grad_middle,
+    grad_own,
+    w_grads,
+    x_in,
+    query_full,
+    query_t,
+    key_t,
+    key_n,
+    value_n,
+    w_qkv_in,
+    logsum,
+    tokens_out,
+    mlp_out,
+    qkv_out,
+    sums_out,
+    x_all,
+    grad_att,
+    grads_t,
+    sum_keys,
+    sum_values,
+    sum_scale,
+    w_own,
+    w_core,
+    w_y,
+    w_x,
+    w_z,
+    w_far,
+    w_last,
+    dx_own,
+    dx_x,
+    dx_z,
+    dx_z_last,
+    dx_x_last,
+    w_qkv,
+    dw_core,
+    dw_y,
+    dw_far,
+    dw_last,
+    all_sums,
+    got_sums,
+    send_sem,
+    recv_sem,
+    local_sem,
+):
+    place = Place(group)
+    core, y, quarter, half, narrow = (
+        place.core,
+        place.y,
+        place.quarter,
+        place.half,
+        place.narrow,
+    )
+    rows = tokens.shape[0]
+    mid = rows // 2
+    slab = qkv_out.shape[2]
+    cols = qkv_out.shape[3]
+    pair_cols = 2 * cols
+    cols_y = part(y, pair_cols)
+    cols_other = part(1 - y, pair_cols)
+    x_dev, z_dev, far_dev = (
+        place.along_narrow(1),
+        place.along_narrow(2),
+        place.along_narrow(group),
+    )
+    core_dev, y_dev = place.along_wide(1), place.along_wide(2)
+    ids = iter(range(send_sem.shape[0]))
+    sent = []
+    dxs = w_core
+    dw = w_qkv
+
+    def copy(source, target, device, index):
+        return pltpu.make_async_remote_copy(
+            src_ref=source,
+            dst_ref=target,
+            send_sem=send_sem.at[index],
+            recv_sem=recv_sem.at[index],
+            device_id=device,
+            device_id_type=MESH,
+        )
+
+    def exchange(source, target, device):
+        index = next(ids)
+        out = copy(source, target, device, index)
+        out.start()
+        sent.append(out)
+        return out
+
+    greet(place, range(1, group + 1), (1, 2))
+
+    heads = query_t.shape[0]
+    first_id = next(ids)
+    for _ in range(3 * heads - 1):
+        next(ids)
+
+    def att_copy(head, mask, incoming):
+        peer = flip(quarter, mask)
+        index = first_id + 3 * head + mask - 1
+        if incoming:
+            there = grad_att.at[head, :, part(peer, rows)]
+            return copy(there, there, place.along_narrow(mask), index)
+        return copy(
+            grad_own.at[lax.div(head, 2), lax.rem(head, 2), peer],
+            grad_att.at[head, :, part(quarter, rows)],
+            place.along_narrow(mask),
+            index,
+        )
+
+    for head in range(heads):
+        for mask in (3, 1, 2):
+            att_copy(head, mask, False).start()
+        grad_att[head, :, part(quarter, rows)] = grad_own[head // 2, head % 2, quarter]
+    span_m = w_own.shape[1]
+    loads = []
+    m_core = []
+    for m in range(3):
+        m_core.append(
+            exchange(w_grads.at[m, 1 - core], w_core.at[m * span_m : (m + 1) * span_m], core_dev)
+        )
+        loads.append(pltpu.make_async_copy(w_grads.at[m, core], w_own.at[m], local_sem.at[m]))
+        loads[-1].start()
+    late = [
+        pltpu.make_async_copy(source, target, local_sem.at[3 + k])
+        for k, (source, target) in enumerate(
+            ((x_in, x_all), (w_qkv_in, w_qkv), (grad_middle, tokens_out))
+        )
+    ]
+    for one in late:
+        one.start()
+
+    def y_step(m):
+        m_core[m].wait_recv()
+        loads[m].wait()
+        add_rows(w_own.at[m], w_core.at[m * span_m : (m + 1) * span_m], 128)
+        return exchange(w_own.at[m, :, cols_other], w_y.at[m], y_dev)
+
+    def block(m, mask):
+        return (m, part(flip(narrow, mask), slab), cols_y)
+
+    def add_block(m, mask, arrived):
+        where = block(m, mask)
+        w_own[where] = (w_own[where].astype(F32) + arrived.astype(F32)).astype(LOW)
+
+    def x_step(m, arrived):
+        arrived.wait_recv()
+        add_rows(w_own.at[m, :, cols_y], w_y.at[m], 128)
+        return [
+            exchange(w_own.at[block(m, o)], w_x.at[m, (o ^ 1) // 2], x_dev)
+            for o in (1, 3, group + 1, group + 3)
+        ]
+
+    def z_step(m, arrived):
+        for k, one in enumerate(arrived):
+            one.wait_recv()
+        for k in range(4):
+            add_block(m, 2 * k, w_x[m, k])
+        return [
+            exchange(w_own.at[block(m, o)], w_z.at[m, (o ^ 2) // group], z_dev)
+            for o in (2, group + 2)
+        ]
+
+    def far_step(m, arrived):
+        for one in arrived:
+            one.wait_recv()
+        for k in range(2):
+            add_block(m, group * k, w_z[m, k])
+        return exchange(w_own.at[block(m, group)], w_far.at[m], far_dev)
+
+    def last_step(total, out_ref, m, buffer):
+        mine = jnp.where(core == 0, total[:, :cols], total[:, cols:])
+        theirs = jnp.where(core == 0, total[:, cols:], total[:, :cols])
+        out_ref[m, core] = mine
+        buffer[m] = theirs
+        return exchange(buffer.at[m], out_ref.at[m, core], core_dev)
+
+    def m_last(m, arrived):
+        arrived.wait_recv()
+        total = w_own[block(m, 0)].astype(F32) + w_far[m].astype(F32)
+        return last_step(total, mlp_out, m, w_last)
+
+    ends = document_ends(lengths, half)
+    sum_scale[...] = jnp.zeros_like(sum_scale)
+
+    def one_head(head, carry):
+        for mask in (1, 2, 3):
+            att_copy(head, mask, True).wait_recv()
+        backward_head(
+            head,
+            ends,
+            query_t,
+            query_full,
+            key_n,
+            key_t,
+            value_n,
+            grad_att,
+            logsum,
+            scale,
+            grads_t,
+            sum_keys,
+            sum_values,
+            sum_scale,
+        )
+        return carry
+
+    m_y = [y_step(0), y_step(1), y_step(2)]
+    lax.fori_loop(0, heads - 1, one_head, 0)
+    m_x = [x_step(0, m_y[0])]
+    lax.fori_loop(heads - 1, heads, one_head, 0)
+
+    size = 3 * heads * HEAD_DIM
+    for one in late:
+        one.wait()
+
+    def grad_inputs(mask, target, start):
+        first = flip(quarter, mask) * 2
+        for which in range(2):
+            span = part(first + which, mid)
+            there = slice(start + which * mid, start + (which + 1) * mid)
+            target[there] = product(
+                grads_t[:, :, :, span].reshape(size, mid), w_qkv[...].reshape(size, -1), 0, 0
+            ).astype(target.dtype)
+
+    slot = {1: 0, 2: 1, 3: 2}
+
+    def dx_part(mask, which):
+        start = slot[mask] * rows + which * mid
+        return slice(start, start + mid)
+
+    def keep(mask):
+        grad_inputs(mask, dxs, slot[mask] * rows)
+
+    keep(3)
+    from_x1 = exchange(dxs.at[dx_part(3, 0)], dx_x.at[1], x_dev)
+    from_z1 = exchange(dxs.at[dx_part(3, 1)], dx_z.at[1], z_dev)
+    keep(1)
+    from_x0 = exchange(dxs.at[dx_part(1, 0)], dx_x.at[0], x_dev)
+    keep(2)
+    from_z0 = exchange(dxs.at[dx_part(2, 1)], dx_z.at[0], z_dev)
+    grad_inputs(0, dx_own, 0)
+
+    all_sums[0] = sums[...]
+    all_sums[0, 3:4, :HEAD_DIM] = jnp.sum(sum_scale[...].T, axis=0, keepdims=True)
+    for mask in (3, 1, 2, 0):
+        where = flip(quarter, mask)
+        start = slot[mask] * rows if mask else 0
+        grads = dxs.at[start : start + rows] if mask else dx_own
+
+        def gain_rows(span, where=where, grads=grads):
+            inputs = x_all[where, span, :].astype(F32)
+            normed = inputs * norm_rows(inputs)
+            terms = grads[span, :].astype(F32) * normed
+            all_sums[0, 4:5, :] += jnp.sum(terms, axis=0, keepdims=True)
+            x_all[where, span, :] = (normed * gain[...]).astype(LOW)
+
+        chunks(rows, 128, gain_rows)
+
+    sum_devices = [core_dev, y_dev, x_dev, z_dev, far_dev]
+
+    def sum_step(stage):
+        return exchange(all_sums.at[stage], got_sums.at[stage], sum_devices[stage])
+
+    def sum_add(stage, arrived):
+        arrived.wait_recv()
+        all_sums[stage + 1] = all_sums[stage] + got_sums[stage]
+
+    sums_now = sum_step(0)
+    for m in range(3):
+        dw[m] = (
+            product(grads_t[m].reshape(size // 3, LEN), x_all[...].reshape(LEN, -1))
+            .astype(LOW)
+            .reshape(dw.shape[1:])
+        )
+    q_core = exchange(dw.at[:, 1 - core], dw_core, core_dev)
+    sum_add(0, sums_now)
+    sums_now = sum_step(1)
+    q_core.wait_recv()
+    for m in range(3):
+        dw[m, core] = (dw[m, core].astype(F32) + dw_core[m].astype(F32)).astype(LOW)
+    q_y = exchange(dw.at[:, core, :, :, cols_other], dw_y, y_dev)
+
+    from_x1.wait_recv()
+    there = dx_part(2, 0)
+    add_rows(dxs.at[there], dx_x.at[1], 128)
+    from_z2 = exchange(dxs.at[there], dx_z_last, z_dev)
+    from_z1.wait_recv()
+    there = dx_part(1, 1)
+    add_rows(dxs.at[there], dx_z.at[1], 128)
+    from_x2 = exchange(dxs.at[there], dx_x_last, x_dev)
+
+    sum_add(1, sums_now)
+    sums_now = sum_step(2)
+    m_x += [x_step(1, m_y[1])]
+    m_z = [z_step(0, m_x[0])]
+    sum_add(2, sums_now)
+    sums_now = sum_step(3)
+    q_y.wait_recv()
+    here = (slice(None), core, slice(None), slice(None), cols_y)
+    dw[here] = (dw[here].astype(F32) + dw_y[...].astype(F32)).astype(LOW)
+    q_far = exchange(dw.at[:, core, 1 - half, :, cols_y], dw_far, far_dev)
+    m_x += [x_step(2, m_y[2])]
+    m_z += [z_step(1, m_x[1])]
+    m_far = [far_step(0, m_z[0])]
+    sum_add(3, sums_now)
+    sums_now = sum_step(4)
+    m_z += [z_step(2, m_x[2])]
+    m_far += [far_step(1, m_z[1])]
+    q_far.wait_recv()
+    last = []
+    for m in range(3):
+        total = dw[m, core, half, :, cols_y].astype(F32) + dw_far[m].astype(F32)
+        last.append(last_step(total, qkv_out, m, dw_last))
+    last.append(m_last(0, m_far[0]))
+    m_far += [far_step(2, m_z[2])]
+    last.append(m_last(1, m_far[1]))
+    sum_add(4, sums_now)
+    sums_out[...] = all_sums[5]
+
+    from_x0.wait_recv()
+    from_z0.wait_recv()
+    from_z2.wait_recv()
+    from_x2.wait_recv()
+    for which, (first, second) in enumerate(((dx_x, dx_z_last), (dx_z, dx_x_last))):
+
+        def final_rows(span, which=which, first=first, second=second):
+            here = pl.ds(which * mid + span.start, span.size)
+            inputs = tokens[here, :].astype(F32)
+            inverse = norm_rows(inputs)
+            normed = inputs * inverse
+            grad = dx_own[here, :] + first[0, span, :].astype(F32) + second[span, :].astype(F32)
+            scaled = grad * gain[...]
+            inner = jnp.mean(scaled * normed, axis=1, keepdims=True)
+            tokens_out[here, :] += inverse * (scaled - normed * inner)
+
+        chunks(mid, 128, final_rows)
+    last.append(m_last(2, m_far[2]))
+
+    for one in last:
+        one.wait_recv()
+
+    def finish_send(head, carry):
+        for mask in (1, 2, 3):
+            att_copy(head, mask, False).wait_send()
+        return carry
+
+    lax.fori_loop(0, heads, finish_send, 0)
+    for one in sent:
+        one.wait_send()
+
+
+def struct(shape, dtype):
+    return jax.ShapeDtypeStruct(shape, dtype)
+
+
+def kernel_call(kernel, outputs, in_specs, out_spaces, scratch, collective_id=None):
+    extra = {} if collective_id is None else {"collective_id": collective_id, "has_side_effects": True}
+    return pl.pallas_call(
+        kernel,
+        out_shape=tuple(outputs),
+        in_specs=[pl.BlockSpec(memory_space=space) for space in in_specs],
+        out_specs=tuple(pl.BlockSpec(memory_space=space) for space in out_spaces),
+        scratch_shapes=scratch,
+        compiler_params=pltpu.CompilerParams(vmem_limit_bytes=VMEM_LIMIT, **extra),
+    )
+
+
+def fused_device(
+    group,
+    tokens,
+    lengths,
+    qkv_weight,
+    out_weight,
+    up_weight,
+    up_bias,
+    down_weight,
+    down_bias,
+    attn_gain,
+    mlp_gain,
+    query_scale,
+    cotangent,
+):
+    rows, dim = tokens.shape
+    slab2, cols = out_weight.shape
+    slab = slab2 // 2
+    halves = lengths.shape[0]
+    heads = halves * slab2 // HEAD_DIM
+    local = heads * HEAD_DIM
+    narrow_count = group * halves
+    hidden = slab2 * narrow_count
+    vmem, smem, anywhere = pltpu.VMEM, pltpu.SMEM, pl.ANY
+
+    shards = jnp.concatenate(
+        [
+            jnp.swapaxes(qkv_weight, 1, 2),
+            out_weight[None],
+            up_weight.T[None],
+            down_weight[None],
+        ]
+    )
+    gain_one, gain_two = attn_gain[None], mlp_gain[None]
+    scale_dim = LOG_TWO_E / math.sqrt(HEAD_DIM) * jax.nn.softplus(query_scale)
+    scale_one = scale_dim[:, None]
+    scale_all = jnp.tile(scale_one, (heads, 1))
+    bias_rows = jnp.broadcast_to(up_bias.astype(F32)[None], (8, slab2))
+
+    att_shape = (2, halves, group, HEAD_DIM, rows)
+    wq_shape = (3, 2, halves, slab, dim)
+    wm_shape = (3, 2, narrow_count * slab, dim)
+    dma = pltpu.SemaphoreType.DMA
+
+    forward_outputs = [
+        struct((group, rows, dim), LOW),
+        struct((local, LEN), F32),
+        struct((heads, HEAD_DIM, LEN), LOW),
+        struct((heads, HEAD_DIM, LEN), LOW),
+        struct((heads, LEN, HEAD_DIM), LOW),
+        struct((heads, LEN, HEAD_DIM), LOW),
+        struct(wq_shape, LOW),
+        struct((heads, 1, LEN), F32),
+        struct(att_shape, LOW),
+        struct(wm_shape, LOW),
+        struct((narrow_count, 8, slab2), F32),
+    ]
+    x_all, query_full, query_t, key_t, key_n, value_n, w_qkv, logsum, att_all, w_mlp, bias_all = (
+        kernel_call(
+            functools.partial(forward_kernel, group),
+            forward_outputs,
+            [smem] + [vmem] * 5,
+            [anywhere] * len(forward_outputs),
+            [
+                vmem((group, rows, dim), LOW),
+                vmem(wq_shape, LOW),
+                vmem(wm_shape, LOW),
+                vmem((6, slab, 2 * cols), LOW),
+                vmem((6, slab, cols), LOW),
+                vmem((narrow_count, 8, slab2), F32),
+                vmem((local, LEN), F32),
+                vmem((heads, HEAD_DIM, LEN), LOW),
+                vmem((heads, HEAD_DIM, LEN), LOW),
+                vmem((heads, HEAD_DIM, LEN), LOW),
+                vmem((heads, LEN, HEAD_DIM), LOW),
+                vmem((heads, LEN, HEAD_DIM), LOW),
+                vmem((heads, 1, LEN), F32),
+                vmem((heads, HEAD_DIM, LEN), LOW),
+                vmem(att_shape, LOW),
+                dma((64,)),
+                dma((64,)),
+                dma((16,)),
+            ],
+            collective_id=0,
+        )(lengths, tokens, shards, gain_one, scale_all, bias_rows)
+    )
+
+    def hidden_order(values):
+        return values.reshape(narrow_count, 2, slab).swapaxes(0, 1).reshape(1, hidden)
+
+    result, grad_middle, grad_att, w_grads, sums = kernel_call(
+        mlp_kernel,
+        [
+            struct((rows, dim), LOW),
+            struct((rows, dim), F32),
+            struct(att_shape, LOW),
+            struct(wm_shape, LOW),
+            struct((8, dim), F32),
+        ],
+        [vmem] * 7,
+        [vmem] * 5,
+        [],
+    )(
+        tokens,
+        att_all,
+        w_mlp,
+        hidden_order(bias_all[:, 0]),
+        down_bias.astype(F32)[None],
+        gain_two,
+        cotangent,
+    )
+
+    last_shape = (3, 2, slab, cols)
+    grad_tokens, mlp_grads, qkv_grads, totals = kernel_call(
+        functools.partial(backward_kernel, group),
+        [
+            struct((rows, dim), F32),
+            struct(last_shape, F32),
+            struct(last_shape, F32),
+            struct((8, dim), F32),
+        ],
+        [smem] + [vmem] * 4 + [anywhere, vmem] + [anywhere] * 2 + [vmem] * 5 + [anywhere, vmem],
+        [vmem] * 4,
+        [
+            vmem((group, rows, dim), LOW),
+            vmem((heads, HEAD_DIM, LEN), LOW),
+            vmem((3, heads, HEAD_DIM, LEN), LOW),
+            vmem((HEAD_DIM, LEN), F32),
+            vmem((HEAD_DIM, LEN), F32),
+            vmem((HEAD_DIM, TILE // 2), F32),
+            vmem((3, narrow_count * slab, dim), LOW),
+            vmem((3 * narrow_count * slab, dim), LOW),
+            vmem((3, narrow_count * slab, 2 * cols), LOW),
+            vmem((3, 4, slab, 2 * cols), LOW),
+            vmem((3, 2, slab, 2 * cols), LOW),
+            vmem((3, slab, 2 * cols), LOW),
+            vmem((3, slab, cols), F32),
+            vmem((rows, dim), F32),
+            vmem((2, rows // 2, dim), LOW),
+            vmem((2, rows // 2, dim), LOW),
+            vmem((rows // 2, dim), LOW),
+            vmem((rows // 2, dim), LOW),
+            vmem(wq_shape, LOW),
+            vmem((3, halves, slab, dim), LOW),
+            vmem((3, halves, slab, 2 * cols), LOW),
+            vmem((3, slab, 2 * cols), LOW),
+            vmem((3, slab, cols), F32),
+            vmem((6, 8, dim), F32),
+            vmem((5, 8, dim), F32),
+            dma((80,)),
+            dma((80,)),
+            dma((6,)),
+        ],
+        collective_id=1,
+    )(
+        lengths,
+        tokens,
+        gain_one,
+        scale_one,
+        sums,
+        grad_middle,
+        grad_att,
+        w_grads,
+        x_all,
+        query_full,
+        query_t,
+        key_t,
+        key_n,
+        value_n,
+        w_qkv,
+        logsum,
+    )
+
+    mlp_grads = mlp_grads.reshape(3, slab2, cols)
+    grad_up_bias = lax.dynamic_index_in_dim(
+        totals[2].reshape(2, narrow_count, slab), lax.axis_index("narrow"), 1, keepdims=False
+    ).reshape(slab2)
+    grad_scale = (
+        totals[3, :HEAD_DIM] * (LOG_TWO_E / math.sqrt(HEAD_DIM)) * jax.nn.sigmoid(query_scale)
+    )
+    return (
+        result,
+        grad_tokens,
+        jnp.swapaxes(qkv_grads.reshape(3, slab2, cols), 1, 2),
+        mlp_grads[0],
+        mlp_grads[1].T,
+        grad_up_bias,
+        mlp_grads[2],
+        totals[1],
+        totals[4],
+        totals[0],
+        grad_scale,
+    )
+
+
 def solution(mesh):
+    wide_count, narrow_count = mesh.shape["wide"], mesh.shape["narrow"]
+
+    def per_device(*args):
+        tokens, lengths, out_weight = args[0], args[1], args[3]
+        group = LEN // tokens.shape[0]
+        fits = (
+            wide_count == 4
+            and group == 4
+            and narrow_count == group * lengths.shape[0] == 8
+            and out_weight.shape[0] == 2 * HEAD_DIM
+            and 2 * out_weight.shape[1] % 128 == 0
+        )
+        if fits:
+            return fused_device(group, *args)
+        return general_device(*args)
+
     return jax.shard_map(
         per_device,
         mesh=mesh,

time: 2450 us -> 314 us (0.13)
  waiting for transfers between devices: 1920 us -> 0 us
  Pallas kernels: 0 us -> 287 us
  matrix products: 228 us -> 0 us
  local copies, waits for them, and re-layouts: 109 us -> 15.7 us
  other arithmetic: 97.3 us -> 4.1 us
  blocking collectives: 71 us -> 0 us
    reduce_scatter x4 -> x0, waiting for transfers between devices: 1370 us -> none  [group_parts(): return lax.psum_scatter(values, 'narrow', scatter_dimension=0, tiled=True)]
    all_gather x5 -> x0, waiting for transfers between devices: 544 us -> none  [the longest x4 544 us: group_rows(): return lax.all_gather(values, 'narrow', axis=0, tiled=True)]
    pallas_call x0 -> x3, Pallas kernels: none -> 287 us  [the longest x1 136 us: fused_device(): kernel_call(functools.partial(forward_kernel, group), forward_outputs, [s...]
    dot_general x32 -> x0, matrix products: 190 us -> none  [the longest x4 35.9 us: attend_backward(): jnp.einsum('ihd,jhd->hij', grad_block, value_block, preferred_element_typ...]
    psum x2 -> x0, blocking collectives: 48.3 us -> none  [the longest x1 40.9 us: per_device(): lax.psum((grad_attn_gain, grad_mlp_gain, grad_down_bias, grad_scale_part)...]
    unnamed x210 -> x10, local copies, waits for them, and re-layouts: 50.7 us -> 4.35 us
    convert_element_type x10 -> x0, other arithmetic: 42.6 us -> none  [the longest x4 34.7 us: attend_backward(): (soft_probs * (grad_probs - inner_sums[:, :, None])).astype(jnp.bfloat16)]
    unnamed x4 -> x0, matrix products: 37.5 us -> none
  transfers between devices with their start and end apart: 13 -> 0, of which waited for: 9 -> 0; matrix products, arithmetic and copies ran while one was open for 12% -> 0% of each run, Pallas kernels for 0% -> 0%
where the time goes in v1:
time: 314 us; the launch traced here: 308 us
  Pallas kernels  287 us (91%)
  local copies, waits for them, and re-layouts  15.7 us (5%)
  other arithmetic  4.1 us (1%)
    pallas_call x1, Pallas kernels, fused_device(): kernel_call(functools.partial(forward_kernel, group), forward_outputs, [s...  136 us
    pallas_call x1, Pallas kernels, fused_device(): kernel_call(functools.partial(backward_kernel, group), [struct((rows, dim...  125 us
    pallas_call x1, Pallas kernels, fused_device(): kernel_call(mlp_kernel, [struct((rows, dim), LOW), struct((rows, dim), F3...  26 us

profile of v1, /device:TPU:11, one launch (start us, length us, event | category | flops | bytes accessed | tf_op | source)
XLA Modules:
  0.0 307.7 jit_solution(5443258844774316524)
XLA Ops:
  0.6 0.0 copy-start.1
  0.7 0.0 copy-start.2
  0.7 1.3 broadcast_in_dim.32.gain
  2.0 2.2 pad_maximum_fusion.shards
  4.2 0.7 fusion
  4.9 0.8 tile.10.scale
  5.7 1.3 broadcast_in_dim.33.bias
  6.9 136.3 %shard_map.203 = (bf16[4,512,1280]{2,1,0:T(8,128)(2,1)}, f32[320,2048]{1,0:T(8,128)}, bf16[4,80,2048]{2,1,0:T(8,128)(2,1)}, bf16[4,80,2048]{2,1,0:T(8,128)(2,1)}...) custom-call(s32[2,4]{1,0:T(2,128)} %lengths.3, ...), custom_call_target="tpu_custom_call" | custom-call | tf_op jit(solution)/shard_map/pallas_call | solution.py:1221
  143.3 0.9 slice_reduce_fusion
  144.1 0.1 reshape_squeeze.6
  144.2 0.7 reshape.48.up_bias
  144.9 0.0 copy-done.1
  144.9 0.6 broadcast_in_dim.36.gain
  145.5 0.6 reshape.51.down_bias
  146.1 26.0 %shard_map.204 = (bf16[512,1280]{1,0:T(8,128)(2,1)}, f32[512,1280]{1,0:T(8,128)}, bf16[2,2,4,80,512]{4,3,2,1,0:T(8,128)(2,1)}, bf16[3,2,640,1280]{3,2,1,0:T(8,128)(2,1)}, f32[8,1280]{1,0:T(8,128)}) custom-call(bf16[512,1280]{1,0:T(8,128)(2,1)} %tokens.5, bf16[2,2,4,80,512]{4,3,2,1,0:T(8,128)(2,1)} %get-tuple-element.31.attended, ...), custom_call_target="tpu_custom_call" | custom-call | tf_op jit(solution)/shard_map/pallas_call | solution.py:1253
  172.2 0.7 copy.27.scale
  172.9 124.6 %shard_map.205 = (f32[512,1280]{1,0:T(8,128)}, f32[3,2,80,320]{3,2,1,0:T(8,128)}, f32[3,2,80,320]{3,2,1,0:T(8,128)}, f32[8,1280]{1,0:T(8,128)}) custom-call(s32[2,4]{1,0:T(2,128)} %lengths.3, bf16[512,1280]{1,0:T(8,128)(2,1)} %tokens.5, f32[1,1280]{1,0:T(1,128)} %broadcast_in_dim.32.gain, f32[80,1]{1,0:T(8,128)} %copy.27.scale, ...), custom_call_target="tpu_custom_call" | custom-call | tf_op jit(solution)/shard_map/pallas_call | solution.py:1276
  297.5 2.1 fusion.1
  299.5 1.6 slice_reduce_fusion.1
  301.1 0.1 reshape_squeeze.7
  301.2 0.6 reshape.50
  301.9 1.2 divide_multiply_fusion
  303.1 3.5 %copy.32 = f32[512,1280]{1,0:T(8,128)} copy(f32[512,1280]{1,0:T(8,128)} %get-tuple-element.70) | data formatting | bytes 5242880
  306.6 0.9 copy.33
  (9 shorter events, 0.1 us)
Async XLA Ops:
  0.6 144.3 %copy-start.1 = (f32[1280]{0:T(1024)S(1)}, f32[1280]{0:T(1024)}, u32[]{:S(2)}) copy-start(f32[1280]{0:T(1024)} %param.21) | copy-start | bytes 15364
  0.7 144.9 %copy-start.2 = (bf16[1280]{0:T(1024)(128)(2,1)S(1)}, bf16[1280]{0:T(1024)(128)(2,1)}, u32[]{:S(2)}) copy-start(bf16[1280]{0:T(1024)(128)(2,1)} %param.19) | copy-start | bytes 7684
  146.1 26.0 %copy-start.3 = (f32[80]{0:T(128)S(1)}, f32[80]{0:T(128)}, u32[]{:S(2)}) copy-start(f32[80]{0:T(128)} %param.22) | copy-start | bytes 964
  303.1 3.5 %copy-start = (f32[3,2,80,320]{3,2,1,0:T(8,128)S(1)}, f32[3,2,80,320]{3,2,1,0:T(8,128)}, u32[]{:S(2)}) copy-start(f32[3,2,80,320]{3,2,1,0:T(8,128)} %get-tuple-element.48) | copy-start | bytes 1843204
